TPU v7x, 512 devices: a whole 4x8x8 slice. The times are simulated.
512 devices in a mesh: frames: 128 (over z, y, x_lo), heads: 4 (over x_hi, core).
Axes of the slice: x: 4 (x_hi: 2, x_lo: 2; x = x_hi * 2 + x_lo), y: 8, z: 8, core: 2. Of those that a mesh axis runs over, the one named last changes fastest.
Arguments:
- queries: bfloat16 [12288, 2560], P('frames', 'heads'), may hold values from -40 to 40
- keys_values: bfloat16 [2, 12288, 2560], P(None, 'frames', 'heads'), may hold values from -40 to 40
- out_weight: bfloat16 [2560, 5120], P('heads', 'frames'), may hold values from -0.5 to 0.5
Outputs:
- projected: bfloat16 [12288, 5120], P('frames', 'heads')
All inputs are finite; a program needn't handle non-finite values.
Results may differ from a plain program's by a relative error of at most 0.015.
Values may be sent and summed in bfloat16 or wider, within the bound.
A program may use at most 64 MiB of HBM per device.

v0:
```python
import jax
import jax.numpy as jnp
from jax import lax
from jax.sharding import PartitionSpec as P

HD = 128
TPF = 32
FR_DEV = 3
reach_cap = 32


def from_behind(x, axis, by):
    devices = lax.axis_size(axis)
    return lax.ppermute(x, axis, [(i, (i + by) % devices) for i in range(devices)])


def on_device(queries, keys_values, out_weight):
    total_frames = lax.axis_size("frames") * FR_DEV
    reach = min(reach_cap, (total_frames - 1) // 2)
    steps = (reach + FR_DEV - 1) // FR_DEV
    width = keys_values.shape[2]
    span = FR_DEV + 2 * reach
    stacked = keys_values.reshape(2, FR_DEV, TPF, width)
    pieces = []
    for offset in range(-steps, steps + 1):
        if offset == 0:
            pieces.append(stacked)
        else:
            pieces.append(from_behind(stacked, "frames", -offset))
    window = jnp.concatenate(pieces, axis=1)
    lower_frame = steps * FR_DEV - reach
    extended = window[:, lower_frame : lower_frame + span]
    keys_ext = extended[0].reshape(span * TPF, width)
    values_ext = extended[1].reshape(span * TPF, width)
    row_frame = jnp.arange(FR_DEV * TPF, dtype=jnp.int32) // TPF
    col_frame = jnp.arange(span * TPF, dtype=jnp.int32) // TPF
    allowed = (col_frame[None, :] >= row_frame[:, None]) & (
        col_frame[None, :] <= row_frame[:, None] + 2 * reach
    )
    results = []
    for head in range(width // HD):
        lower = head * HD
        query_cols = queries[:, lower : lower + HD]
        key_cols = keys_ext[:, lower : lower + HD]
        scores = lax.dot_general(
            query_cols, key_cols, (((1,), (1,)), ((), ())), preferred_element_type=jnp.float32
        )
        scores = scores * HD ** (-0.5)
        top = jnp.max(jnp.where(allowed, scores, -1e30), axis=1, keepdims=True)
        weights = jnp.where(allowed, jnp.exp(scores - top), 0.0)
        probs = (weights / jnp.sum(weights, axis=1, keepdims=True)).astype(jnp.bfloat16)
        results.append(
            jnp.dot(
                probs, values_ext[:, lower : lower + HD], preferred_element_type=jnp.float32
            ).astype(jnp.bfloat16)
        )
    attended = jnp.concatenate(results, axis=1)
    partial_rows = jnp.dot(
        attended,
        lax.all_gather(out_weight, "frames", axis=1, tiled=True),
        preferred_element_type=jnp.float32,
    )
    return lax.psum_scatter(
        partial_rows.astype(jnp.bfloat16), "heads", scatter_dimension=1, tiled=True
    )


def solution(mesh):
    in_specs = (P("frames", "heads"), P(None, "frames", "heads"), P("heads", "frames"))
    out_specs = P("frames", "heads")
    return jax.shard_map(
        on_device, mesh=mesh, in_specs=in_specs, out_specs=out_specs, check_vma=False
    )
```

profile of v0, /device:TPU:1, one launch (start us, length us, event | category | flops | bytes accessed | tf_op | source)
XLA Modules:
  0.0 740.1 jit_solution(7605853426506819960)
XLA Ops:
  6.5 0.7 all-gather.2.cloned.1.call-update
  7.3 8.4 %collective-permute-start = (bf16[2,3,32,640]{3,2,1,0:T(8,128)(2,1)}, bf16[2,3,32,640]{3,2,1,0:T(8,128)(2,1)S(1)}, u32[]{:S(2)}, u32[]{:S(2)}) collective-permute-start(bf16[2,3,32,640]{3,2,1,0:T(8,128)(2,1)} %bitcast.25), channel_id=1, source_target_pairs={{0,44},{4,48},{8,52},{12,56},{16,60},{20,64},{24,68},{28,72},{32,7... | collective-permute-start | bytes 737288 | tf_op jit(solution)/shard_map/ppermute | solution.py:14
  15.7 4.6 collective-permute-start.1
  20.3 4.8 collective-permute-start.2
  25.2 6.2 collective-permute-start.3
  31.4 4.4 collective-permute-start.4
  35.8 4.3 collective-permute-start.5
  40.2 8.4 %collective-permute-done.1 = bf16[2,3,32,640]{3,2,1,0:T(8,128)(2,1)S(1)} collective-permute-done((bf16[2,3,32,640]{3,2,1,0:T(8,128)(2,1)}, bf16[2,3,32,640]{3,2,1,0:T(8,128)(2,1)S(1)}, u32[]{:S(2)}, u32[]{:S(2)}) %collective-permute-start.1) | collective-permute-done | bytes 245792 | tf_op jit(solution)/shard_map/ppermute | solution.py:14
  48.6 6.4 collective-permute-start.6
  55.0 6.1 collective-permute-done.2
  61.1 19.7 %collective-permute-start.7 = (bf16[2,3,32,640]{3,2,1,0:T(8,128)(2,1)}, bf16[2,3,32,640]{3,2,1,0:T(8,128)(2,1)S(1)}, u32[]{:S(2)}, u32[]{:S(2)}) collective-permute-start(bf16[2,3,32,640]{3,2,1,0:T(8,128)(2,1)} %bitcast.32), channel_id=1, source_target_pairs={{0,16},{4,20},{8,24},{12,28},{16,32},{20,36},{24,40},{28,44},{32,4... | collective-permute-start | bytes 737288 | tf_op jit(solution)/shard_map/ppermute | solution.py:14
  80.8 6.9 collective-permute-start.8
  87.8 6.6 collective-permute-start.9
  94.4 1.9 collective-permute-start.10
  96.4 7.6 %collective-permute-start.11 = (bf16[2,3,32,640]{3,2,1,0:T(8,128)(2,1)}, bf16[2,3,32,640]{3,2,1,0:T(8,128)(2,1)S(1)}, u32[]{:S(2)}, u32[]{:S(2)}) collective-permute-start(bf16[2,3,32,640]{3,2,1,0:T(8,128)(2,1)} %bitcast.36), channel_id=1, source_target_pairs={{0,508},{4,0},{8,4},{12,8},{16,12},{20,16},{24,20},{28,24},{32,28}... | collective-permute-start | bytes 737288 | tf_op jit(solution)/shard_map/ppermute | solution.py:14
  104.0 2.6 collective-permute-done.7
  106.6 7.4 %collective-permute-start.12 = (bf16[2,3,32,640]{3,2,1,0:T(8,128)(2,1)}, bf16[2,3,32,640]{3,2,1,0:T(8,128)(2,1)S(1)}, u32[]{:S(2)}, u32[]{:S(2)}) collective-permute-start(bf16[2,3,32,640]{3,2,1,0:T(8,128)(2,1)} %bitcast.37), channel_id=1, source_target_pairs={{0,504},{4,508},{8,0},{12,4},{16,8},{20,12},{24,16},{28,20},{32,24... | collective-permute-start | bytes 737288 | tf_op jit(solution)/shard_map/ppermute | solution.py:14
  114.1 2.5 collective-permute-done.8
  116.6 3.8 collective-permute-start.13
  120.4 5.2 collective-permute-start.14
  125.7 6.7 collective-permute-done.10
  132.4 1.9 collective-permute-start.15
  134.3 1.0 constant_dynamic-update-slice_fusion.11
  135.3 7.5 %collective-permute-start.16 = (bf16[2,3,32,640]{3,2,1,0:T(8,128)(2,1)S(1)}, bf16[2,3,32,640]{3,2,1,0:T(8,128)(2,1)S(1)}, u32[]{:S(2)}, u32[]{:S(2)}) collective-permute-start(bf16[2,3,32,640]{3,2,1,0:T(8,128)(2,1)S(1)} %bitcast.42), channel_id=1, source_target_pairs={{0,488},{4,492},{8,496},{12,500},{16,504},{20,508},{24,0},{28,4},{... | collective-permute-start | bytes 737288 | tf_op jit(solution)/shard_map/ppermute | solution.py:14
  142.9 7.3 collective-permute-start.17
  150.3 1.9 collective-permute-start.18
  152.3 2.9 collective-permute-start.19
  155.2 8.1 %collective-permute-start.20 = (bf16[2,3,32,640]{3,2,1,0:T(8,128)(2,1)S(1)}, bf16[2,3,32,640]{3,2,1,0:T(8,128)(2,1)S(1)}, u32[]{:S(2)}, u32[]{:S(2)}) collective-permute-start(bf16[2,3,32,640]{3,2,1,0:T(8,128)(2,1)S(1)} %bitcast.46), channel_id=1, source_target_pairs={{0,472},{4,476},{8,480},{12,484},{16,488},{20,492},{24,496},{28,50... | collective-permute-start | bytes 737288 | tf_op jit(solution)/shard_map/ppermute | solution.py:14
  163.3 9.2 %collective-permute-done.16 = bf16[2,3,32,640]{3,2,1,0:T(8,128)(2,1)S(1)} collective-permute-done((bf16[2,3,32,640]{3,2,1,0:T(8,128)(2,1)S(1)}, bf16[2,3,32,640]{3,2,1,0:T(8,128)(2,1)S(1)}, u32[]{:S(2)}, u32[]{:S(2)}) %collective-permute-start.16) | collective-permute-done | bytes 245792 | tf_op jit(solution)/shard_map/ppermute | solution.py:14
  172.5 1.9 collective-permute-start.21
  174.5 6.0 collective-permute-done.17
  180.6 32.5 %collective-permute-done.20 = bf16[2,3,32,640]{3,2,1,0:T(8,128)(2,1)S(1)} collective-permute-done((bf16[2,3,32,640]{3,2,1,0:T(8,128)(2,1)S(1)}, bf16[2,3,32,640]{3,2,1,0:T(8,128)(2,1)S(1)}, u32[]{:S(2)}, u32[]{:S(2)}) %collective-permute-start.20) | collective-permute-done | bytes 245792 | tf_op jit(solution)/shard_map/ppermute | solution.py:14
  213.3 0.5 fusion.38
  213.8 0.4 copy-done.1
  214.1 0.3 fusion
  214.4 0.3 fusion.2
  214.8 0.3 fusion.3
  215.1 0.5 select_reduce_fusion
  215.6 1.0 fusion.14
  216.6 0.7 fusion.13
  217.3 0.4 fusion.9
  217.7 0.4 fusion.8
  218.2 0.4 fusion.7
  218.6 0.4 fusion.6
  219.1 0.5 fusion.5
  219.5 395.4 %all-gather.2.cloned.1.call-done = bf16[640,5120]{0,1:T(8,128)(2,1)} async-done(((bf16[640,40]{0,1:T(8,128)(2,1)}), bf16[640,5120]{0,1:T(8,128)(2,1)}) %all-gather.2.cloned.1.call-update) | async-done | bytes 6553616 | tf_op jit(solution)/shard_map/all_gather | solution.py:60
  614.9 5.9 convolution_convert_fusion
  620.9 112.4 %reduce-scatter.2.cloned.1.call-done = bf16[96,1280]{1,0:T(8,128)(2,1)} async-done(((bf16[96,5120]{1,0:T(8,128)(2,1)}), bf16[96,1280]{1,0:T(8,128)(2,1)}) %reduce-scatter.2.cloned.1.call-update) | async-done | bytes 245776 | tf_op jit(solution)/shard_map/reduce_scatter | solution.py:63
  (44 shorter events, 0.8 us)
Async XLA Ops:
  6.5 128.8 %copy-start = (bf16[2,96,640]{2,1,0:T(8,128)(2,1)S(1)}, bf16[2,96,640]{2,1,0:T(8,128)(2,1)}, u32[]{:S(2)}) copy-start(bf16[2,96,640]{2,1,0:T(8,128)(2,1)} %param.4) | copy-start | bytes 737284
  6.5 608.4 %all-gather.2.cloned.1.call-start = ((), (), s32[]{:S(2)}) async-start(), calls=%async_computation.1 | async-start | bytes 6604800 | tf_op jit(solution)/shard_map/all_gather | solution.py:60
  7.3 726.0 %reduce-scatter.2.cloned.1.call-start = ((), (), s32[]{:S(2)}) async-start(), calls=%async_computation.2 | async-start | bytes 1228800 | tf_op jit(solution)/shard_map/reduce_scatter | solution.py:63
  7.3 28.5 %collective-permute-start = (bf16[2,3,32,640]{3,2,1,0:T(8,128)(2,1)}, bf16[2,3,32,640]{3,2,1,0:T(8,128)(2,1)S(1)}, u32[]{:S(2)}, u32[]{:S(2)}) collective-permute-start(bf16[2,3,32,640]{3,2,1,0:T(8,128)(2,1)} %bitcast.25), channel_id=1, source_target_pairs={{0,44},{4,48},{8,52},{12,56},{16,60},{20,64},{24,68},{28,72},{32,7... | collective-permute-start | bytes 737288 | tf_op jit(solution)/shard_map/ppermute | solution.py:14
  15.7 32.9 %collective-permute-start.1 = (bf16[2,3,32,640]{3,2,1,0:T(8,128)(2,1)}, bf16[2,3,32,640]{3,2,1,0:T(8,128)(2,1)S(1)}, u32[]{:S(2)}, u32[]{:S(2)}) collective-permute-start(bf16[2,3,32,640]{3,2,1,0:T(8,128)(2,1)} %bitcast.26), channel_id=1, source_target_pairs={{0,40},{4,44},{8,48},{12,52},{16,56},{20,60},{24,64},{28,68},{32,7... | collective-permute-start | bytes 737288 | tf_op jit(solution)/shard_map/ppermute | solution.py:14
  20.3 40.8 %collective-permute-start.2 = (bf16[2,3,32,640]{3,2,1,0:T(8,128)(2,1)}, bf16[2,3,32,640]{3,2,1,0:T(8,128)(2,1)S(1)}, u32[]{:S(2)}, u32[]{:S(2)}) collective-permute-start(bf16[2,3,32,640]{3,2,1,0:T(8,128)(2,1)} %bitcast.27), channel_id=1, source_target_pairs={{0,36},{4,40},{8,44},{12,48},{16,52},{20,56},{24,60},{28,64},{32,6... | collective-permute-start | bytes 737288 | tf_op jit(solution)/shard_map/ppermute | solution.py:14
  25.2 55.7 %collective-permute-start.3 = (bf16[2,3,32,640]{3,2,1,0:T(8,128)(2,1)}, bf16[2,3,32,640]{3,2,1,0:T(8,128)(2,1)S(1)}, u32[]{:S(2)}, u32[]{:S(2)}) collective-permute-start(bf16[2,3,32,640]{3,2,1,0:T(8,128)(2,1)} %bitcast.28), channel_id=1, source_target_pairs={{0,32},{4,36},{8,40},{12,44},{16,48},{20,52},{24,56},{28,60},{32,6... | collective-permute-start | bytes 737288 | tf_op jit(solution)/shard_map/ppermute | solution.py:14
  31.4 56.4 %collective-permute-start.4 = (bf16[2,3,32,640]{3,2,1,0:T(8,128)(2,1)}, bf16[2,3,32,640]{3,2,1,0:T(8,128)(2,1)S(1)}, u32[]{:S(2)}, u32[]{:S(2)}) collective-permute-start(bf16[2,3,32,640]{3,2,1,0:T(8,128)(2,1)} %bitcast.29), channel_id=1, source_target_pairs={{0,28},{4,32},{8,36},{12,40},{16,44},{20,48},{24,52},{28,56},{32,6... | collective-permute-start | bytes 737288 | tf_op jit(solution)/shard_map/ppermute | solution.py:14
  35.8 58.6 %collective-permute-start.5 = (bf16[2,3,32,640]{3,2,1,0:T(8,128)(2,1)}, bf16[2,3,32,640]{3,2,1,0:T(8,128)(2,1)S(1)}, u32[]{:S(2)}, u32[]{:S(2)}) collective-permute-start(bf16[2,3,32,640]{3,2,1,0:T(8,128)(2,1)} %bitcast.30), channel_id=1, source_target_pairs={{0,24},{4,28},{8,32},{12,36},{16,40},{20,44},{24,48},{28,52},{32,5... | collective-permute-start | bytes 737288 | tf_op jit(solution)/shard_map/ppermute | solution.py:14
  48.6 47.8 %collective-permute-start.6 = (bf16[2,3,32,640]{3,2,1,0:T(8,128)(2,1)}, bf16[2,3,32,640]{3,2,1,0:T(8,128)(2,1)S(1)}, u32[]{:S(2)}, u32[]{:S(2)}) collective-permute-start(bf16[2,3,32,640]{3,2,1,0:T(8,128)(2,1)} %bitcast.31), channel_id=1, source_target_pairs={{0,20},{4,24},{8,28},{12,32},{16,36},{20,40},{24,44},{28,48},{32,5... | collective-permute-start | bytes 737288 | tf_op jit(solution)/shard_map/ppermute | solution.py:14
  61.1 45.5 %collective-permute-start.7 = (bf16[2,3,32,640]{3,2,1,0:T(8,128)(2,1)}, bf16[2,3,32,640]{3,2,1,0:T(8,128)(2,1)S(1)}, u32[]{:S(2)}, u32[]{:S(2)}) collective-permute-start(bf16[2,3,32,640]{3,2,1,0:T(8,128)(2,1)} %bitcast.32), channel_id=1, source_target_pairs={{0,16},{4,20},{8,24},{12,28},{16,32},{20,36},{24,40},{28,44},{32,4... | collective-permute-start | bytes 737288 | tf_op jit(solution)/shard_map/ppermute | solution.py:14
  80.8 35.7 %collective-permute-start.8 = (bf16[2,3,32,640]{3,2,1,0:T(8,128)(2,1)}, bf16[2,3,32,640]{3,2,1,0:T(8,128)(2,1)S(1)}, u32[]{:S(2)}, u32[]{:S(2)}) collective-permute-start(bf16[2,3,32,640]{3,2,1,0:T(8,128)(2,1)} %bitcast.33), channel_id=1, source_target_pairs={{0,12},{4,16},{8,20},{12,24},{16,28},{20,32},{24,36},{28,40},{32,4... | collective-permute-start | bytes 737288 | tf_op jit(solution)/shard_map/ppermute | solution.py:14
  87.8 32.6 %collective-permute-start.9 = (bf16[2,3,32,640]{3,2,1,0:T(8,128)(2,1)}, bf16[2,3,32,640]{3,2,1,0:T(8,128)(2,1)S(1)}, u32[]{:S(2)}, u32[]{:S(2)}) collective-permute-start(bf16[2,3,32,640]{3,2,1,0:T(8,128)(2,1)} %bitcast.34), channel_id=1, source_target_pairs={{0,8},{4,12},{8,16},{12,20},{16,24},{20,28},{24,32},{28,36},{32,40... | collective-permute-start | bytes 737288 | tf_op jit(solution)/shard_map/ppermute | solution.py:14
  94.4 37.9 %collective-permute-start.10 = (bf16[2,3,32,640]{3,2,1,0:T(8,128)(2,1)}, bf16[2,3,32,640]{3,2,1,0:T(8,128)(2,1)S(1)}, u32[]{:S(2)}, u32[]{:S(2)}) collective-permute-start(bf16[2,3,32,640]{3,2,1,0:T(8,128)(2,1)} %bitcast.35), channel_id=1, source_target_pairs={{0,4},{4,8},{8,12},{12,16},{16,20},{20,24},{24,28},{28,32},{32,36}... | collective-permute-start | bytes 737288 | tf_op jit(solution)/shard_map/ppermute | solution.py:14
  96.4 38.9 %collective-permute-start.11 = (bf16[2,3,32,640]{3,2,1,0:T(8,128)(2,1)}, bf16[2,3,32,640]{3,2,1,0:T(8,128)(2,1)S(1)}, u32[]{:S(2)}, u32[]{:S(2)}) collective-permute-start(bf16[2,3,32,640]{3,2,1,0:T(8,128)(2,1)} %bitcast.36), channel_id=1, source_target_pairs={{0,508},{4,0},{8,4},{12,8},{16,12},{20,16},{24,20},{28,24},{32,28}... | collective-permute-start | bytes 737288 | tf_op jit(solution)/shard_map/ppermute | solution.py:14
  106.6 36.3 %collective-permute-start.12 = (bf16[2,3,32,640]{3,2,1,0:T(8,128)(2,1)}, bf16[2,3,32,640]{3,2,1,0:T(8,128)(2,1)S(1)}, u32[]{:S(2)}, u32[]{:S(2)}) collective-permute-start(bf16[2,3,32,640]{3,2,1,0:T(8,128)(2,1)} %bitcast.37), channel_id=1, source_target_pairs={{0,504},{4,508},{8,0},{12,4},{16,8},{20,12},{24,16},{28,20},{32,24... | collective-permute-start | bytes 737288 | tf_op jit(solution)/shard_map/ppermute | solution.py:14
  116.6 33.7 %collective-permute-start.13 = (bf16[2,3,32,640]{3,2,1,0:T(8,128)(2,1)}, bf16[2,3,32,640]{3,2,1,0:T(8,128)(2,1)S(1)}, u32[]{:S(2)}, u32[]{:S(2)}) collective-permute-start(bf16[2,3,32,640]{3,2,1,0:T(8,128)(2,1)} %bitcast.38), channel_id=1, source_target_pairs={{0,500},{4,504},{8,508},{12,0},{16,4},{20,8},{24,12},{28,16},{32,2... | collective-permute-start | bytes 737288 | tf_op jit(solution)/shard_map/ppermute | solution.py:14
  120.4 31.9 %collective-permute-start.14 = (bf16[2,3,32,640]{3,2,1,0:T(8,128)(2,1)}, bf16[2,3,32,640]{3,2,1,0:T(8,128)(2,1)S(1)}, u32[]{:S(2)}, u32[]{:S(2)}) collective-permute-start(bf16[2,3,32,640]{3,2,1,0:T(8,128)(2,1)} %bitcast.39), channel_id=1, source_target_pairs={{0,496},{4,500},{8,504},{12,508},{16,0},{20,4},{24,8},{28,12},{32,... | collective-permute-start | bytes 737288 | tf_op jit(solution)/shard_map/ppermute | solution.py:14
  132.4 22.8 %collective-permute-start.15 = (bf16[2,3,32,640]{3,2,1,0:T(8,128)(2,1)}, bf16[2,3,32,640]{3,2,1,0:T(8,128)(2,1)S(1)}, u32[]{:S(2)}, u32[]{:S(2)}) collective-permute-start(bf16[2,3,32,640]{3,2,1,0:T(8,128)(2,1)} %bitcast.40), channel_id=1, source_target_pairs={{0,492},{4,496},{8,500},{12,504},{16,508},{20,0},{24,4},{28,8},{32... | collective-permute-start | bytes 737288 | tf_op jit(solution)/shard_map/ppermute | solution.py:14
  135.3 37.2 %collective-permute-start.16 = (bf16[2,3,32,640]{3,2,1,0:T(8,128)(2,1)S(1)}, bf16[2,3,32,640]{3,2,1,0:T(8,128)(2,1)S(1)}, u32[]{:S(2)}, u32[]{:S(2)}) collective-permute-start(bf16[2,3,32,640]{3,2,1,0:T(8,128)(2,1)S(1)} %bitcast.42), channel_id=1, source_target_pairs={{0,488},{4,492},{8,496},{12,500},{16,504},{20,508},{24,0},{28,4},{... | collective-permute-start | bytes 737288 | tf_op jit(solution)/shard_map/ppermute | solution.py:14
  142.9 37.6 %collective-permute-start.17 = (bf16[2,3,32,640]{3,2,1,0:T(8,128)(2,1)S(1)}, bf16[2,3,32,640]{3,2,1,0:T(8,128)(2,1)S(1)}, u32[]{:S(2)}, u32[]{:S(2)}) collective-permute-start(bf16[2,3,32,640]{3,2,1,0:T(8,128)(2,1)S(1)} %bitcast.43), channel_id=1, source_target_pairs={{0,484},{4,488},{8,492},{12,496},{16,500},{20,504},{24,508},{28,0}... | collective-permute-start | bytes 737288 | tf_op jit(solution)/shard_map/ppermute | solution.py:14
  150.3 30.3 %collective-permute-start.18 = (bf16[2,3,32,640]{3,2,1,0:T(8,128)(2,1)S(1)}, bf16[2,3,32,640]{3,2,1,0:T(8,128)(2,1)S(1)}, u32[]{:S(2)}, u32[]{:S(2)}) collective-permute-start(bf16[2,3,32,640]{3,2,1,0:T(8,128)(2,1)S(1)} %bitcast.44), channel_id=1, source_target_pairs={{0,480},{4,484},{8,488},{12,492},{16,496},{20,500},{24,504},{28,50... | collective-permute-start | bytes 737288 | tf_op jit(solution)/shard_map/ppermute | solution.py:14
  152.3 28.3 %collective-permute-start.19 = (bf16[2,3,32,640]{3,2,1,0:T(8,128)(2,1)S(1)}, bf16[2,3,32,640]{3,2,1,0:T(8,128)(2,1)S(1)}, u32[]{:S(2)}, u32[]{:S(2)}) collective-permute-start(bf16[2,3,32,640]{3,2,1,0:T(8,128)(2,1)S(1)} %bitcast.45), channel_id=1, source_target_pairs={{0,476},{4,480},{8,484},{12,488},{16,492},{20,496},{24,500},{28,50... | collective-permute-start | bytes 737288 | tf_op jit(solution)/shard_map/ppermute | solution.py:14
  155.2 58.0 %collective-permute-start.20 = (bf16[2,3,32,640]{3,2,1,0:T(8,128)(2,1)S(1)}, bf16[2,3,32,640]{3,2,1,0:T(8,128)(2,1)S(1)}, u32[]{:S(2)}, u32[]{:S(2)}) collective-permute-start(bf16[2,3,32,640]{3,2,1,0:T(8,128)(2,1)S(1)} %bitcast.46), channel_id=1, source_target_pairs={{0,472},{4,476},{8,480},{12,484},{16,488},{20,492},{24,496},{28,50... | collective-permute-start | bytes 737288 | tf_op jit(solution)/shard_map/ppermute | solution.py:14
  172.5 40.7 %collective-permute-start.21 = (bf16[2,3,32,640]{3,2,1,0:T(8,128)(2,1)S(1)}, bf16[2,3,32,640]{3,2,1,0:T(8,128)(2,1)S(1)}, u32[]{:S(2)}, u32[]{:S(2)}) collective-permute-start(bf16[2,3,32,640]{3,2,1,0:T(8,128)(2,1)S(1)} %bitcast.47), channel_id=1, source_target_pairs={{0,468},{4,472},{8,476},{12,480},{16,484},{20,488},{24,492},{28,49... | collective-permute-start | bytes 737288 | tf_op jit(solution)/shard_map/ppermute | solution.py:14
  213.2 0.9 copy-start.1
Sparse Core Ops, SparseCore 0:
  9.4 605.4 all-gather.1
  621.0 112.2 reduce-scatter.1
where the time goes:
time: 741 us; the launch traced here: 740 us
  waiting for transfers between devices  582 us (79%)
  starting transfers between devices  130 us (18%)
  between operations  14 us (2%)
  matrix products  10.6 us (1%)
    all_gather x1, waiting for transfers between devices, on_device(): lax.all_gather(out_weight, 'frames', axis=1, tiled=True)  395 us
    ppermute x22, starting transfers between devices, from_behind(): lax.ppermute(x, axis, [(i, (i + by) % devices) for i in range(devices)])  130 us
    reduce_scatter x1, waiting for transfers between devices, on_device(): lax.psum_scatter(partial_rows.astype(jnp.bfloat16), 'heads', scatter_dime...  112 us
    ppermute x22, waiting for transfers between devices, from_behind(): lax.ppermute(x, axis, [(i, (i + by) % devices) for i in range(devices)])  74 us
  transfers between devices with their start and end apart: 24, of which 10 were waited for; matrix products, arithmetic and copies ran while one was open for 1% of the time, Pallas kernels for 0%

commit v1 on v0

--- a/solution.py
+++ b/solution.py
@@ -57,7 +57,10 @@
     attended = jnp.concatenate(results, axis=1)
     partial_rows = jnp.dot(
         attended,
-        lax.all_gather(out_weight, "frames", axis=1, tiled=True),
+        jnp.concatenate(
+            lax.all_to_all(jnp.stack([out_weight] * lax.axis_size("frames")), "frames", 0, 0),
+            axis=1,
+        ),
         preferred_element_type=jnp.float32,
     )
     return lax.psum_scatter(

time: 741 us -> 473 us (0.64)
  waiting for transfers between devices: 582 us -> 288 us
  starting transfers between devices: 130 us -> 154 us
    all_gather x1 -> x0, waiting for transfers between devices: 395 us -> none  [on_device(): lax.all_gather(out_weight, 'frames', axis=1, tiled=True)]
    ppermute x22, waiting for transfers between devices: 74 us -> 226 us  [from_behind(): lax.ppermute(x, axis, [(i, (i + by) % devices) for i in range(devices)])]
    reduce_scatter x1, waiting for transfers between devices: 112 us -> 62.4 us  [on_device(): lax.psum_scatter(partial_rows.astype(jnp.bfloat16), 'heads', scatter_dime...]
    all_to_all x0 -> x1, starting transfers between devices: none -> 19.9 us  [on_device(): lax.all_to_all(jnp.stack([out_weight] * lax.axis_size('frames')), 'frames...]
  transfers between devices with their start and end apart: 24 -> 24, of which waited for: 10 -> 13; matrix products, arithmetic and copies ran while one was open for 1% -> 1% of each run, Pallas kernels for 0% -> 0%
where the time goes in v1:
time: 473 us
  waiting for transfers between devices  288 us (61%)
  starting transfers between devices  154 us (33%)
  between operations  13.9 us (3%)
  matrix products  10.6 us (2%)
  local copies, waits for them, and re-layouts  5.23 us (1%)
    ppermute x22, waiting for transfers between devices, from_behind(): lax.ppermute(x, axis, [(i, (i + by) % devices) for i in range(devices)])  226 us
    ppermute x22, starting transfers between devices, from_behind(): lax.ppermute(x, axis, [(i, (i + by) % devices) for i in range(devices)])  134 us
    reduce_scatter x1, waiting for transfers between devices, on_device(): lax.psum_scatter(partial_rows.astype(jnp.bfloat16), 'heads', scatter_dime...  62.4 us
    all_to_all x1, starting transfers between devices, on_device(): lax.all_to_all(jnp.stack([out_weight] * lax.axis_size('frames')), 'frames...  19.9 us
  transfers between devices with their start and end apart: 24, of which 13 were waited for; matrix products, arithmetic and copies ran while one was open for 1% of the time, Pallas kernels for 0%

profile of v1, /device:TPU:1, one launch (start us, length us, event | category | flops | bytes accessed | tf_op | source)
XLA Modules:
  0.0 472.5 jit_solution(2914670286374518467)
XLA Ops:
  6.5 4.0 stack.2
  10.6 19.9 %all-to-all-start = ((bf16[128,640,40]{1,2,0:T(8,128)(2,1)}), bf16[128,640,40]{1,2,0:T(8,128)(2,1)}, u32[]{:S(2)}, u32[]{:S(2)}) async-start(bf16[128,640,40]{1,2,0:T(8,128)(2,1)} %stack.2), calls=%async_computation | async-start | bytes 13107200 | tf_op jit(solution)/shard_map/all_to_all | solution.py:61
  30.5 6.3 %collective-permute-start = (bf16[2,3,32,640]{3,2,1,0:T(8,128)(2,1)S(1)}, bf16[2,3,32,640]{3,2,1,0:T(8,128)(2,1)S(1)}, u32[]{:S(2)}, u32[]{:S(2)}) collective-permute-start(bf16[2,3,32,640]{3,2,1,0:T(8,128)(2,1)S(1)} %bitcast.28), channel_id=1, source_target_pairs={{0,44},{4,48},{8,52},{12,56},{16,60},{20,64},{24,68},{28,72},{32,7... | collective-permute-start | bytes 737288 | tf_op jit(solution)/shard_map/ppermute | solution.py:14
  36.8 4.0 collective-permute-start.1
  40.9 4.4 collective-permute-start.2
  45.2 5.8 %collective-permute-start.3 = (bf16[2,3,32,640]{3,2,1,0:T(8,128)(2,1)S(1)}, bf16[2,3,32,640]{3,2,1,0:T(8,128)(2,1)S(1)}, u32[]{:S(2)}, u32[]{:S(2)}) collective-permute-start(bf16[2,3,32,640]{3,2,1,0:T(8,128)(2,1)S(1)} %bitcast.31), channel_id=1, source_target_pairs={{0,32},{4,36},{8,40},{12,44},{16,48},{20,52},{24,56},{28,60},{32,6... | collective-permute-start | bytes 737288 | tf_op jit(solution)/shard_map/ppermute | solution.py:14
  51.1 4.0 collective-permute-start.4
  55.1 134.2 %collective-permute-done = bf16[2,3,32,640]{3,2,1,0:T(8,128)(2,1)S(1)} collective-permute-done((bf16[2,3,32,640]{3,2,1,0:T(8,128)(2,1)S(1)}, bf16[2,3,32,640]{3,2,1,0:T(8,128)(2,1)S(1)}, u32[]{:S(2)}, u32[]{:S(2)}) %collective-permute-start) | collective-permute-done | bytes 245792 | tf_op jit(solution)/shard_map/ppermute | solution.py:14
  189.4 1.9 collective-permute-start.5
  191.3 36.0 %collective-permute-done.1 = bf16[2,3,32,640]{3,2,1,0:T(8,128)(2,1)S(1)} collective-permute-done((bf16[2,3,32,640]{3,2,1,0:T(8,128)(2,1)S(1)}, bf16[2,3,32,640]{3,2,1,0:T(8,128)(2,1)S(1)}, u32[]{:S(2)}, u32[]{:S(2)}) %collective-permute-start.1) | collective-permute-done | bytes 245792 | tf_op jit(solution)/shard_map/ppermute | solution.py:14
  227.3 1.9 collective-permute-start.6
  229.3 8.1 %collective-permute-done.2 = bf16[2,3,32,640]{3,2,1,0:T(8,128)(2,1)S(1)} collective-permute-done((bf16[2,3,32,640]{3,2,1,0:T(8,128)(2,1)S(1)}, bf16[2,3,32,640]{3,2,1,0:T(8,128)(2,1)S(1)}, u32[]{:S(2)}, u32[]{:S(2)}) %collective-permute-start.2) | collective-permute-done | bytes 245792 | tf_op jit(solution)/shard_map/ppermute | solution.py:14
  237.4 7.7 %collective-permute-start.7 = (bf16[2,3,32,640]{3,2,1,0:T(8,128)(2,1)S(1)}, bf16[2,3,32,640]{3,2,1,0:T(8,128)(2,1)S(1)}, u32[]{:S(2)}, u32[]{:S(2)}) collective-permute-start(bf16[2,3,32,640]{3,2,1,0:T(8,128)(2,1)S(1)} %bitcast.35), channel_id=1, source_target_pairs={{0,16},{4,20},{8,24},{12,28},{16,32},{20,36},{24,40},{28,44},{32,4... | collective-permute-start | bytes 737288 | tf_op jit(solution)/shard_map/ppermute | solution.py:14
  245.1 2.9 collective-permute-start.8
  248.1 2.2 collective-permute-done.4
  250.2 7.1 %collective-permute-start.9 = (bf16[2,3,32,640]{3,2,1,0:T(8,128)(2,1)S(1)}, bf16[2,3,32,640]{3,2,1,0:T(8,128)(2,1)S(1)}, u32[]{:S(2)}, u32[]{:S(2)}) collective-permute-start(bf16[2,3,32,640]{3,2,1,0:T(8,128)(2,1)S(1)} %bitcast.37), channel_id=1, source_target_pairs={{0,8},{4,12},{8,16},{12,20},{16,24},{20,28},{24,32},{28,36},{32,40... | collective-permute-start | bytes 737288 | tf_op jit(solution)/shard_map/ppermute | solution.py:14
  257.4 1.2 collective-permute-done.5
  258.6 1.9 collective-permute-start.10
  260.6 4.7 collective-permute-done.6
  265.3 2.8 collective-permute-start.11
  268.2 2.4 collective-permute-done.7
  270.6 1.9 collective-permute-start.12
  272.5 3.3 collective-permute-done.8
  275.8 9.6 %collective-permute-start.13 = (bf16[2,3,32,640]{3,2,1,0:T(8,128)(2,1)S(1)}, bf16[2,3,32,640]{3,2,1,0:T(8,128)(2,1)S(1)}, u32[]{:S(2)}, u32[]{:S(2)}) collective-permute-start(bf16[2,3,32,640]{3,2,1,0:T(8,128)(2,1)S(1)} %bitcast.41), channel_id=1, source_target_pairs={{0,500},{4,504},{8,508},{12,0},{16,4},{20,8},{24,12},{28,16},{32,2... | collective-permute-start | bytes 737288 | tf_op jit(solution)/shard_map/ppermute | solution.py:14
  285.5 5.6 %collective-permute-start.14 = (bf16[2,3,32,640]{3,2,1,0:T(8,128)(2,1)S(1)}, bf16[2,3,32,640]{3,2,1,0:T(8,128)(2,1)S(1)}, u32[]{:S(2)}, u32[]{:S(2)}) collective-permute-start(bf16[2,3,32,640]{3,2,1,0:T(8,128)(2,1)S(1)} %bitcast.42), channel_id=1, source_target_pairs={{0,496},{4,500},{8,504},{12,508},{16,0},{20,4},{24,8},{28,12},{32,... | collective-permute-start | bytes 737288 | tf_op jit(solution)/shard_map/ppermute | solution.py:14
  291.2 2.1 collective-permute-done.10
  293.3 10.7 %collective-permute-start.15 = (bf16[2,3,32,640]{3,2,1,0:T(8,128)(2,1)S(1)}, bf16[2,3,32,640]{3,2,1,0:T(8,128)(2,1)S(1)}, u32[]{:S(2)}, u32[]{:S(2)}) collective-permute-start(bf16[2,3,32,640]{3,2,1,0:T(8,128)(2,1)S(1)} %bitcast.43), channel_id=1, source_target_pairs={{0,492},{4,496},{8,500},{12,504},{16,508},{20,0},{24,4},{28,8},{32... | collective-permute-start | bytes 737288 | tf_op jit(solution)/shard_map/ppermute | solution.py:14
  304.1 4.9 %collective-permute-start.16 = (bf16[2,3,32,640]{3,2,1,0:T(8,128)(2,1)S(1)}, bf16[2,3,32,640]{3,2,1,0:T(8,128)(2,1)S(1)}, u32[]{:S(2)}, u32[]{:S(2)}) collective-permute-start(bf16[2,3,32,640]{3,2,1,0:T(8,128)(2,1)S(1)} %bitcast.45), channel_id=1, source_target_pairs={{0,488},{4,492},{8,496},{12,500},{16,504},{20,508},{24,0},{28,4},{... | collective-permute-start | bytes 737288 | tf_op jit(solution)/shard_map/ppermute | solution.py:14
  309.1 11.4 %collective-permute-start.17 = (bf16[2,3,32,640]{3,2,1,0:T(8,128)(2,1)S(1)}, bf16[2,3,32,640]{3,2,1,0:T(8,128)(2,1)S(1)}, u32[]{:S(2)}, u32[]{:S(2)}) collective-permute-start(bf16[2,3,32,640]{3,2,1,0:T(8,128)(2,1)S(1)} %bitcast.46), channel_id=1, source_target_pairs={{0,484},{4,488},{8,492},{12,496},{16,500},{20,504},{24,508},{28,0}... | collective-permute-start | bytes 737288 | tf_op jit(solution)/shard_map/ppermute | solution.py:14
  320.6 5.1 %collective-permute-start.18 = (bf16[2,3,32,640]{3,2,1,0:T(8,128)(2,1)S(1)}, bf16[2,3,32,640]{3,2,1,0:T(8,128)(2,1)S(1)}, u32[]{:S(2)}, u32[]{:S(2)}) collective-permute-start(bf16[2,3,32,640]{3,2,1,0:T(8,128)(2,1)S(1)} %bitcast.47), channel_id=1, source_target_pairs={{0,480},{4,484},{8,488},{12,492},{16,496},{20,500},{24,504},{28,50... | collective-permute-start | bytes 737288 | tf_op jit(solution)/shard_map/ppermute | solution.py:14
  325.8 14.9 %collective-permute-start.19 = (bf16[2,3,32,640]{3,2,1,0:T(8,128)(2,1)S(1)}, bf16[2,3,32,640]{3,2,1,0:T(8,128)(2,1)S(1)}, u32[]{:S(2)}, u32[]{:S(2)}) collective-permute-start(bf16[2,3,32,640]{3,2,1,0:T(8,128)(2,1)S(1)} %bitcast.48), channel_id=1, source_target_pairs={{0,476},{4,480},{8,484},{12,488},{16,492},{20,496},{24,500},{28,50... | collective-permute-start | bytes 737288 | tf_op jit(solution)/shard_map/ppermute | solution.py:14
  340.7 3.0 collective-permute-start.20
  343.8 16.1 %collective-permute-start.21 = (bf16[2,3,32,640]{3,2,1,0:T(8,128)(2,1)S(1)}, bf16[2,3,32,640]{3,2,1,0:T(8,128)(2,1)S(1)}, u32[]{:S(2)}, u32[]{:S(2)}) collective-permute-start(bf16[2,3,32,640]{3,2,1,0:T(8,128)(2,1)S(1)} %bitcast.50), channel_id=1, source_target_pairs={{0,468},{4,472},{8,476},{12,480},{16,484},{20,488},{24,492},{28,49... | collective-permute-start | bytes 737288 | tf_op jit(solution)/shard_map/ppermute | solution.py:14
  360.0 4.8 %collective-permute-done.19 = bf16[2,3,32,640]{3,2,1,0:T(8,128)(2,1)S(1)} collective-permute-done((bf16[2,3,32,640]{3,2,1,0:T(8,128)(2,1)S(1)}, bf16[2,3,32,640]{3,2,1,0:T(8,128)(2,1)S(1)}, u32[]{:S(2)}, u32[]{:S(2)}) %collective-permute-start.19) | collective-permute-done | bytes 245792 | tf_op jit(solution)/shard_map/ppermute | solution.py:14
  364.8 16.5 %collective-permute-done.20 = bf16[2,3,32,640]{3,2,1,0:T(8,128)(2,1)S(1)} collective-permute-done((bf16[2,3,32,640]{3,2,1,0:T(8,128)(2,1)S(1)}, bf16[2,3,32,640]{3,2,1,0:T(8,128)(2,1)S(1)}, u32[]{:S(2)}, u32[]{:S(2)}) %collective-permute-start.20) | collective-permute-done | bytes 245792 | tf_op jit(solution)/shard_map/ppermute | solution.py:14
  381.3 10.0 %collective-permute-done.21 = bf16[2,3,32,640]{3,2,1,0:T(8,128)(2,1)S(1)} collective-permute-done((bf16[2,3,32,640]{3,2,1,0:T(8,128)(2,1)S(1)}, bf16[2,3,32,640]{3,2,1,0:T(8,128)(2,1)S(1)}, u32[]{:S(2)}, u32[]{:S(2)}) %collective-permute-start.21) | collective-permute-done | bytes 245792 | tf_op jit(solution)/shard_map/ppermute | solution.py:14
  391.4 0.5 fusion.38
  392.2 0.3 fusion.2
  392.9 0.5 select_reduce_fusion
  393.4 1.0 fusion.14
  394.3 0.7 fusion.13
  395.1 0.4 fusion.9
  395.5 0.4 fusion.8
  396.0 0.4 fusion.7
  396.4 0.4 fusion.6
  396.9 0.5 fusion.5
  397.3 5.9 %convolution_convert_fusion = bf16[96,5120]{1,0:T(8,128)(2,1)} fusion(bf16[96,640]{1,0:T(8,128)(2,1)S(1)} %fusion.5, bf16[640,5120]{0,1:T(8,128)(2,1)} %bitcast.9), kind=kOutput, calls=%fused_computation | convolution fusion | flops 629637120 | bytes 7659520 | tf_op jit(solution)/shard_map/dot_general | solution.py:58
  403.3 62.4 %reduce-scatter.2.cloned.1.call-done = bf16[96,1280]{1,0:T(8,128)(2,1)} async-done(((bf16[96,5120]{1,0:T(8,128)(2,1)}), bf16[96,1280]{1,0:T(8,128)(2,1)}) %reduce-scatter.2.cloned.1.call-update) | async-done | bytes 245776 | tf_op jit(solution)/shard_map/reduce_scatter | solution.py:66
  (44 shorter events, 1.5 us)
Async XLA Ops:
  10.5 19.9 %copy-start = (bf16[2,96,640]{2,1,0:T(8,128)(2,1)S(1)}, bf16[2,96,640]{2,1,0:T(8,128)(2,1)}, u32[]{:S(2)}) copy-start(bf16[2,96,640]{2,1,0:T(8,128)(2,1)} %param.4) | copy-start | bytes 737284
  10.6 386.8 %all-to-all-start = ((bf16[128,640,40]{1,2,0:T(8,128)(2,1)}), bf16[128,640,40]{1,2,0:T(8,128)(2,1)}, u32[]{:S(2)}, u32[]{:S(2)}) async-start(bf16[128,640,40]{1,2,0:T(8,128)(2,1)} %stack.2), calls=%async_computation | async-start | bytes 13107200 | tf_op jit(solution)/shard_map/all_to_all | solution.py:61
  30.4 435.3 %reduce-scatter.2.cloned.1.call-start = ((), (), s32[]{:S(2)}) async-start(), calls=%async_computation.2 | async-start | bytes 1228800 | tf_op jit(solution)/shard_map/reduce_scatter | solution.py:66
  30.5 158.9 %collective-permute-start = (bf16[2,3,32,640]{3,2,1,0:T(8,128)(2,1)S(1)}, bf16[2,3,32,640]{3,2,1,0:T(8,128)(2,1)S(1)}, u32[]{:S(2)}, u32[]{:S(2)}) collective-permute-start(bf16[2,3,32,640]{3,2,1,0:T(8,128)(2,1)S(1)} %bitcast.28), channel_id=1, source_target_pairs={{0,44},{4,48},{8,52},{12,56},{16,60},{20,64},{24,68},{28,72},{32,7... | collective-permute-start | bytes 737288 | tf_op jit(solution)/shard_map/ppermute | solution.py:14
  36.8 190.5 %collective-permute-start.1 = (bf16[2,3,32,640]{3,2,1,0:T(8,128)(2,1)S(1)}, bf16[2,3,32,640]{3,2,1,0:T(8,128)(2,1)S(1)}, u32[]{:S(2)}, u32[]{:S(2)}) collective-permute-start(bf16[2,3,32,640]{3,2,1,0:T(8,128)(2,1)S(1)} %bitcast.29), channel_id=1, source_target_pairs={{0,40},{4,44},{8,48},{12,52},{16,56},{20,60},{24,64},{28,68},{32,7... | collective-permute-start | bytes 737288 | tf_op jit(solution)/shard_map/ppermute | solution.py:14
  40.9 196.6 %collective-permute-start.2 = (bf16[2,3,32,640]{3,2,1,0:T(8,128)(2,1)S(1)}, bf16[2,3,32,640]{3,2,1,0:T(8,128)(2,1)S(1)}, u32[]{:S(2)}, u32[]{:S(2)}) collective-permute-start(bf16[2,3,32,640]{3,2,1,0:T(8,128)(2,1)S(1)} %bitcast.30), channel_id=1, source_target_pairs={{0,36},{4,40},{8,44},{12,48},{16,52},{20,56},{24,60},{28,64},{32,6... | collective-permute-start | bytes 737288 | tf_op jit(solution)/shard_map/ppermute | solution.py:14
  45.2 199.9 %collective-permute-start.3 = (bf16[2,3,32,640]{3,2,1,0:T(8,128)(2,1)S(1)}, bf16[2,3,32,640]{3,2,1,0:T(8,128)(2,1)S(1)}, u32[]{:S(2)}, u32[]{:S(2)}) collective-permute-start(bf16[2,3,32,640]{3,2,1,0:T(8,128)(2,1)S(1)} %bitcast.31), channel_id=1, source_target_pairs={{0,32},{4,36},{8,40},{12,44},{16,48},{20,52},{24,56},{28,60},{32,6... | collective-permute-start | bytes 737288 | tf_op jit(solution)/shard_map/ppermute | solution.py:14
  51.1 199.2 %collective-permute-start.4 = (bf16[2,3,32,640]{3,2,1,0:T(8,128)(2,1)S(1)}, bf16[2,3,32,640]{3,2,1,0:T(8,128)(2,1)S(1)}, u32[]{:S(2)}, u32[]{:S(2)}) collective-permute-start(bf16[2,3,32,640]{3,2,1,0:T(8,128)(2,1)S(1)} %bitcast.32), channel_id=1, source_target_pairs={{0,28},{4,32},{8,36},{12,40},{16,44},{20,48},{24,52},{28,56},{32,6... | collective-permute-start | bytes 737288 | tf_op jit(solution)/shard_map/ppermute | solution.py:14
  189.4 69.2 %collective-permute-start.5 = (bf16[2,3,32,640]{3,2,1,0:T(8,128)(2,1)S(1)}, bf16[2,3,32,640]{3,2,1,0:T(8,128)(2,1)S(1)}, u32[]{:S(2)}, u32[]{:S(2)}) collective-permute-start(bf16[2,3,32,640]{3,2,1,0:T(8,128)(2,1)S(1)} %bitcast.33), channel_id=1, source_target_pairs={{0,24},{4,28},{8,32},{12,36},{16,40},{20,44},{24,48},{28,52},{32,5... | collective-permute-start | bytes 737288 | tf_op jit(solution)/shard_map/ppermute | solution.py:14
  227.3 38.0 %collective-permute-start.6 = (bf16[2,3,32,640]{3,2,1,0:T(8,128)(2,1)S(1)}, bf16[2,3,32,640]{3,2,1,0:T(8,128)(2,1)S(1)}, u32[]{:S(2)}, u32[]{:S(2)}) collective-permute-start(bf16[2,3,32,640]{3,2,1,0:T(8,128)(2,1)S(1)} %bitcast.34), channel_id=1, source_target_pairs={{0,20},{4,24},{8,28},{12,32},{16,36},{20,40},{24,44},{28,48},{32,5... | collective-permute-start | bytes 737288 | tf_op jit(solution)/shard_map/ppermute | solution.py:14
  237.4 33.2 %collective-permute-start.7 = (bf16[2,3,32,640]{3,2,1,0:T(8,128)(2,1)S(1)}, bf16[2,3,32,640]{3,2,1,0:T(8,128)(2,1)S(1)}, u32[]{:S(2)}, u32[]{:S(2)}) collective-permute-start(bf16[2,3,32,640]{3,2,1,0:T(8,128)(2,1)S(1)} %bitcast.35), channel_id=1, source_target_pairs={{0,16},{4,20},{8,24},{12,28},{16,32},{20,36},{24,40},{28,44},{32,4... | collective-permute-start | bytes 737288 | tf_op jit(solution)/shard_map/ppermute | solution.py:14
  245.1 30.7 %collective-permute-start.8 = (bf16[2,3,32,640]{3,2,1,0:T(8,128)(2,1)S(1)}, bf16[2,3,32,640]{3,2,1,0:T(8,128)(2,1)S(1)}, u32[]{:S(2)}, u32[]{:S(2)}) collective-permute-start(bf16[2,3,32,640]{3,2,1,0:T(8,128)(2,1)S(1)} %bitcast.36), channel_id=1, source_target_pairs={{0,12},{4,16},{8,20},{12,24},{16,28},{20,32},{24,36},{28,40},{32,4... | collective-permute-start | bytes 737288 | tf_op jit(solution)/shard_map/ppermute | solution.py:14
  250.2 35.3 %collective-permute-start.9 = (bf16[2,3,32,640]{3,2,1,0:T(8,128)(2,1)S(1)}, bf16[2,3,32,640]{3,2,1,0:T(8,128)(2,1)S(1)}, u32[]{:S(2)}, u32[]{:S(2)}) collective-permute-start(bf16[2,3,32,640]{3,2,1,0:T(8,128)(2,1)S(1)} %bitcast.37), channel_id=1, source_target_pairs={{0,8},{4,12},{8,16},{12,20},{16,24},{20,28},{24,32},{28,36},{32,40... | collective-permute-start | bytes 737288 | tf_op jit(solution)/shard_map/ppermute | solution.py:14
  258.6 34.7 %collective-permute-start.10 = (bf16[2,3,32,640]{3,2,1,0:T(8,128)(2,1)S(1)}, bf16[2,3,32,640]{3,2,1,0:T(8,128)(2,1)S(1)}, u32[]{:S(2)}, u32[]{:S(2)}) collective-permute-start(bf16[2,3,32,640]{3,2,1,0:T(8,128)(2,1)S(1)} %bitcast.38), channel_id=1, source_target_pairs={{0,4},{4,8},{8,12},{12,16},{16,20},{20,24},{24,28},{28,32},{32,36}... | collective-permute-start | bytes 737288 | tf_op jit(solution)/shard_map/ppermute | solution.py:14
  265.3 38.8 %collective-permute-start.11 = (bf16[2,3,32,640]{3,2,1,0:T(8,128)(2,1)S(1)}, bf16[2,3,32,640]{3,2,1,0:T(8,128)(2,1)S(1)}, u32[]{:S(2)}, u32[]{:S(2)}) collective-permute-start(bf16[2,3,32,640]{3,2,1,0:T(8,128)(2,1)S(1)} %bitcast.39), channel_id=1, source_target_pairs={{0,508},{4,0},{8,4},{12,8},{16,12},{20,16},{24,20},{28,24},{32,28}... | collective-permute-start | bytes 737288 | tf_op jit(solution)/shard_map/ppermute | solution.py:14
  270.6 38.5 %collective-permute-start.12 = (bf16[2,3,32,640]{3,2,1,0:T(8,128)(2,1)S(1)}, bf16[2,3,32,640]{3,2,1,0:T(8,128)(2,1)S(1)}, u32[]{:S(2)}, u32[]{:S(2)}) collective-permute-start(bf16[2,3,32,640]{3,2,1,0:T(8,128)(2,1)S(1)} %bitcast.40), channel_id=1, source_target_pairs={{0,504},{4,508},{8,0},{12,4},{16,8},{20,12},{24,16},{28,20},{32,24... | collective-permute-start | bytes 737288 | tf_op jit(solution)/shard_map/ppermute | solution.py:14
  275.8 44.7 %collective-permute-start.13 = (bf16[2,3,32,640]{3,2,1,0:T(8,128)(2,1)S(1)}, bf16[2,3,32,640]{3,2,1,0:T(8,128)(2,1)S(1)}, u32[]{:S(2)}, u32[]{:S(2)}) collective-permute-start(bf16[2,3,32,640]{3,2,1,0:T(8,128)(2,1)S(1)} %bitcast.41), channel_id=1, source_target_pairs={{0,500},{4,504},{8,508},{12,0},{16,4},{20,8},{24,12},{28,16},{32,2... | collective-permute-start | bytes 737288 | tf_op jit(solution)/shard_map/ppermute | solution.py:14
  285.5 40.2 %collective-permute-start.14 = (bf16[2,3,32,640]{3,2,1,0:T(8,128)(2,1)S(1)}, bf16[2,3,32,640]{3,2,1,0:T(8,128)(2,1)S(1)}, u32[]{:S(2)}, u32[]{:S(2)}) collective-permute-start(bf16[2,3,32,640]{3,2,1,0:T(8,128)(2,1)S(1)} %bitcast.42), channel_id=1, source_target_pairs={{0,496},{4,500},{8,504},{12,508},{16,0},{20,4},{24,8},{28,12},{32,... | collective-permute-start | bytes 737288 | tf_op jit(solution)/shard_map/ppermute | solution.py:14
  293.3 47.4 %collective-permute-start.15 = (bf16[2,3,32,640]{3,2,1,0:T(8,128)(2,1)S(1)}, bf16[2,3,32,640]{3,2,1,0:T(8,128)(2,1)S(1)}, u32[]{:S(2)}, u32[]{:S(2)}) collective-permute-start(bf16[2,3,32,640]{3,2,1,0:T(8,128)(2,1)S(1)} %bitcast.43), channel_id=1, source_target_pairs={{0,492},{4,496},{8,500},{12,504},{16,508},{20,0},{24,4},{28,8},{32... | collective-permute-start | bytes 737288 | tf_op jit(solution)/shard_map/ppermute | solution.py:14
  304.1 39.6 %collective-permute-start.16 = (bf16[2,3,32,640]{3,2,1,0:T(8,128)(2,1)S(1)}, bf16[2,3,32,640]{3,2,1,0:T(8,128)(2,1)S(1)}, u32[]{:S(2)}, u32[]{:S(2)}) collective-permute-start(bf16[2,3,32,640]{3,2,1,0:T(8,128)(2,1)S(1)} %bitcast.45), channel_id=1, source_target_pairs={{0,488},{4,492},{8,496},{12,500},{16,504},{20,508},{24,0},{28,4},{... | collective-permute-start | bytes 737288 | tf_op jit(solution)/shard_map/ppermute | solution.py:14
  309.1 50.8 %collective-permute-start.17 = (bf16[2,3,32,640]{3,2,1,0:T(8,128)(2,1)S(1)}, bf16[2,3,32,640]{3,2,1,0:T(8,128)(2,1)S(1)}, u32[]{:S(2)}, u32[]{:S(2)}) collective-permute-start(bf16[2,3,32,640]{3,2,1,0:T(8,128)(2,1)S(1)} %bitcast.46), channel_id=1, source_target_pairs={{0,484},{4,488},{8,492},{12,496},{16,500},{20,504},{24,508},{28,0}... | collective-permute-start | bytes 737288 | tf_op jit(solution)/shard_map/ppermute | solution.py:14
  320.6 39.4 %collective-permute-start.18 = (bf16[2,3,32,640]{3,2,1,0:T(8,128)(2,1)S(1)}, bf16[2,3,32,640]{3,2,1,0:T(8,128)(2,1)S(1)}, u32[]{:S(2)}, u32[]{:S(2)}) collective-permute-start(bf16[2,3,32,640]{3,2,1,0:T(8,128)(2,1)S(1)} %bitcast.47), channel_id=1, source_target_pairs={{0,480},{4,484},{8,488},{12,492},{16,496},{20,500},{24,504},{28,50... | collective-permute-start | bytes 737288 | tf_op jit(solution)/shard_map/ppermute | solution.py:14
  325.8 39.0 %collective-permute-start.19 = (bf16[2,3,32,640]{3,2,1,0:T(8,128)(2,1)S(1)}, bf16[2,3,32,640]{3,2,1,0:T(8,128)(2,1)S(1)}, u32[]{:S(2)}, u32[]{:S(2)}) collective-permute-start(bf16[2,3,32,640]{3,2,1,0:T(8,128)(2,1)S(1)} %bitcast.48), channel_id=1, source_target_pairs={{0,476},{4,480},{8,484},{12,488},{16,492},{20,496},{24,500},{28,50... | collective-permute-start | bytes 737288 | tf_op jit(solution)/shard_map/ppermute | solution.py:14
  340.7 40.6 %collective-permute-start.20 = (bf16[2,3,32,640]{3,2,1,0:T(8,128)(2,1)S(1)}, bf16[2,3,32,640]{3,2,1,0:T(8,128)(2,1)S(1)}, u32[]{:S(2)}, u32[]{:S(2)}) collective-permute-start(bf16[2,3,32,640]{3,2,1,0:T(8,128)(2,1)S(1)} %bitcast.49), channel_id=1, source_target_pairs={{0,472},{4,476},{8,480},{12,484},{16,488},{20,492},{24,496},{28,50... | collective-permute-start | bytes 737288 | tf_op jit(solution)/shard_map/ppermute | solution.py:14
  343.8 47.6 %collective-permute-start.21 = (bf16[2,3,32,640]{3,2,1,0:T(8,128)(2,1)S(1)}, bf16[2,3,32,640]{3,2,1,0:T(8,128)(2,1)S(1)}, u32[]{:S(2)}, u32[]{:S(2)}) collective-permute-start(bf16[2,3,32,640]{3,2,1,0:T(8,128)(2,1)S(1)} %bitcast.50), channel_id=1, source_target_pairs={{0,468},{4,472},{8,476},{12,480},{16,484},{20,488},{24,492},{28,49... | collective-permute-start | bytes 737288 | tf_op jit(solution)/shard_map/ppermute | solution.py:14
  381.3 10.6 %copy-start.1 = (bf16[96,640]{1,0:T(8,128)(2,1)S(1)}, bf16[96,640]{1,0:T(8,128)(2,1)}, u32[]{:S(2)}) copy-start(bf16[96,640]{1,0:T(8,128)(2,1)} %param.3) | copy-start | bytes 368644
Sparse Core Ops, SparseCore 0:
  403.4 62.2 reduce-scatter.1
